TPU v7x, 128 devices: a whole 4x4x4 slice. The times are simulated.
128 devices in a mesh: gx: 16 (over y, z), gy: 8 (over x, core).
Axes of the slice: x: 4, y: 4, z: 4, core: 2. Of those that a mesh axis runs over, the one named last changes fastest.
Arguments:
- probes: bfloat16 [16, 131072], P(None, ('gx', 'gy')), may hold values from -73 to 73, as said below
- previous: bfloat16 [16, 131072], P(None, ('gx', 'gy')), may hold values from -6 to 6
- prev_coupling: float32 [16, 16], replicated, may hold values from -1.5 to 1.5
- leaves: bfloat16 [128, 1024, 1024], P(('gx', 'gy')), may hold values from -1 to 3, as said below
- bases: bfloat16 [7, 64, 131072], P(None, None, ('gx', 'gy')), may hold values from -6 to 6
- leaf_sizes: int32 [128], P(('gx', 'gy')), may hold values from 1 to 1024, 98304 in all
Outputs:
- rayleigh: float32 [16, 16], replicated
- factor: float32 [16, 16], replicated
- next_block: float32 [16, 131072], P(None, ('gx', 'gy'))
Inputs may be any that keep to these rules, and one draw needn't show every extreme that they name: For every probe p and slot s, |probes[p, s]| stays within the range below. Each leaves[i] is symmetric. `leaf_sizes`: the real points of a leaf fill its first slots; the sizes sum to 98304.
All inputs are finite; a program needn't handle non-finite values. No bound on the sum of `leaf_sizes` on one device may be relied on, other than what follows from the above.
Results may differ from a plain program's by a relative error of at most 0.0022.
Values sent between devices are 32-bit elements; how exact they have to be, the bound alone decides.
No kernel may reach another device: no remote copies, remote signals or barrier semaphores. Data moves between devices by JAX's collectives and lax.ppermute only.
A program may use at most 64 MiB of HBM per device.

v0:
```python
import math
import jax
import jax.numpy as jnp
from jax import lax
from jax.sharding import Mesh
from jax.sharding import PartitionSpec as P

GX_GY = ("gx_0", "gx_1", "gy_0", "gy_1")


def partner_2(block, axis, stride):
    count = lax.axis_size(axis)
    route = []
    for low in range(count):
        high = low | 1 << stride
        if high != low and high < count:
            route += [(low, high), (high, low)]
    return lax.ppermute(block, axis, route)


def one_axis_at_a_time(value, axes):
    for axis in axes:
        value = lax.psum(value, axis)
    return value


def sibling_sums(partials, spread):
    results = []
    remaining = partials
    for bit_number in range(spread):
        received = partner_2(remaining, GX_GY, bit_number)
        results.append(received[0])
        remaining = remaining[1:] + received[1:]
    return results


def body(probes, previous, prev_coupling, leaves, bases, leaf_sizes):
    highest = lax.Precision.HIGHEST
    probe_count = probes.shape[0]
    leaf_count = leaves.shape[0]
    leaf_rows = leaves.shape[1]
    rows = leaf_count * leaf_rows
    rank = bases.shape[1]
    devices = lax.axis_size(GX_GY)
    spread = devices.bit_length() - 1
    filled = leaf_count * devices * leaf_rows * 3 // 4
    inverse = 1.0 / filled
    valid = (jnp.arange(leaf_rows, dtype=jnp.int32)[None, :] < leaf_sizes[:, None]).reshape(rows)
    block = jnp.where(valid[None, :], probes, jnp.zeros_like(probes))
    older = jnp.where(valid[None, :], previous, jnp.zeros_like(previous))
    shaped = block.reshape(probe_count, leaf_count, leaf_rows)
    image = jnp.einsum("lrc,plc->plr", leaves, shaped, preferred_element_type=jnp.float32).reshape(
        probe_count, rows
    )
    partials = jnp.einsum("pm,krm->kpr", block, bases, preferred_element_type=jnp.float32)
    partners = sibling_sums(partials, spread)
    for bit_number in range(spread):
        width = rows * 2**bit_number
        scaled = (partners[bit_number] * (1.0 / math.sqrt(rank * width))).astype(jnp.bfloat16)
        image = image + jnp.dot(scaled, bases[bit_number], preferred_element_type=jnp.float32)
    image = jnp.where(valid[None, :], image, jnp.zeros_like(image))
    dense = block.astype(jnp.float32)
    older_dense = older.astype(jnp.float32)
    stacked = jnp.concatenate([image, dense, older_dense], 0)
    joint = one_axis_at_a_time(jnp.dot(stacked, stacked.T, precision=highest) * inverse, GX_GY)
    rayleigh = joint[probe_count : 2 * probe_count, :probe_count]
    mixing = jnp.concatenate(
        [jnp.eye(probe_count, dtype=jnp.float32), -rayleigh.T, -prev_coupling], 1
    )
    gram = jnp.dot(jnp.dot(mixing, joint, precision=highest), mixing.T, precision=highest)
    residual = (
        image
        - jnp.dot(rayleigh.T, dense, precision=highest)
        - jnp.dot(prev_coupling, older_dense, precision=highest)
    )
    factor = jnp.linalg.cholesky(gram)
    next_block = jax.scipy.linalg.solve_triangular(factor, residual, lower=True)
    return (rayleigh, factor, next_block)


def solution(mesh):
    split = Mesh(mesh.devices.reshape(4, 4, 4, 2), ("gx_0", "gx_1", "gy_0", "gy_1"))
    return jax.shard_map(
        body,
        mesh=split,
        in_specs=(
            P(None, GX_GY),
            P(None, GX_GY),
            P(),
            P(GX_GY, None, None),
            P(None, None, GX_GY),
            P(GX_GY),
        ),
        out_specs=(P(), P(), P(None, GX_GY)),
        check_vma=False,
    )
```

profile of v0, /device:TPU:1, one launch (start us, length us, event | category | flops | bytes accessed | tf_op | source)
XLA Modules:
  0.0 97.7 jit_solution(13078462689037245916)
XLA Ops:
  0.6 0.0 copy-start
  0.6 0.0 copy-start.1
  0.7 0.0 copy-start.2
  0.7 0.0 copy-start.3
  0.7 0.0 copy-start.4
  1.5 1.7 %convolution_bitcast_fusion.1 = f32[7,16,64]{2,1,0:T(8,128)S(1)} fusion(bf16[7,64,1024]{2,1,0:T(8,128)(2,1)} %param.10, bf16[16,1024]{1,0:T(8,128)(2,1)} %param.6, pred[1024]{0:T(1024)(128)(4,1)S(1)} %iota_compare_fusion.2), kind=kOutput, calls=%fused_computation.13 | convolution fusion | flops 14696448 | bytes 979968 | tf_op jit(solution)/shard_map/pm,krm->kpr/dot_general | solution.py:55
  3.2 1.5 %collective-permute-start = (f32[7,16,64]{2,1,0:T(8,128)S(1)}, f32[7,16,64]{2,1,0:T(8,128)S(1)}, u32[]{:S(2)}, u32[]{:S(2)}) collective-permute-start(f32[7,16,64]{2,1,0:T(8,128)S(1)} %convolution_bitcast_fusion.1), channel_id=1, source_target_pairs={{0,1},{1,0},{2,3},{3,2},{4,5},{5,4},{6,7},{7,6},{8,9},{9,8},{10,11... | collective-permute-start | bytes 86024 | tf_op jit(solution)/shard_map/ppermute | solution.py:18
  4.7 0.0 copy-done
  4.7 1.4 %fusion = f32[16,1024]{1,0:T(8,128)S(1)} fusion(bf16[1,1024,1024]{2,1,0:T(8,128)(2,1)S(1)} %copy-done, bf16[16,1024]{1,0:T(8,128)(2,1)} %param.6, pred[1024]{0:T(1024)(128)(4,1)S(1)} %iota_compare_fusion.2), kind=kOutput, calls=%fused_computation | convolution fusion | flops 33570816 | bytes 2196480 | tf_op jit(solution)/shard_map/lrc,plc->plr/dot_general | solution.py:52
  6.1 0.0 copy-done.2
  6.1 0.0 copy-done.3
  6.2 0.0 copy-done.4
  6.2 0.0 collective-permute-done
  6.2 1.4 %collective-permute-start.1 = (f32[6,16,64]{2,1,0:T(8,128)S(1)}, f32[6,16,64]{2,1,0:T(8,128)S(1)}, u32[]{:S(2)}, u32[]{:S(2)}) collective-permute-start(f32[6,16,64]{2,1,0:T(8,128)S(1)} %slice_add_fusion), channel_id=1, source_target_pairs={{0,2},{2,0},{1,3},{3,1},{4,6},{6,4},{5,7},{7,5},{8,10},{10,8},{9,1... | collective-permute-start | bytes 73736 | tf_op jit(solution)/shard_map/ppermute | solution.py:18
  7.6 0.0 copy-done.1
  7.6 0.1 convolution_add_fusion.6
  7.7 1.9 %collective-permute-done.1 = f32[6,16,64]{2,1,0:T(8,128)S(1)} collective-permute-done((f32[6,16,64]{2,1,0:T(8,128)S(1)}, f32[6,16,64]{2,1,0:T(8,128)S(1)}, u32[]{:S(2)}, u32[]{:S(2)}) %collective-permute-start.1) | collective-permute-done | bytes 24608 | tf_op jit(solution)/shard_map/ppermute | solution.py:18
  9.7 2.8 %collective-permute-start.2 = (f32[5,16,64]{2,1,0:T(8,128)S(1)}, f32[5,16,64]{2,1,0:T(8,128)S(1)}, u32[]{:S(2)}, u32[]{:S(2)}) collective-permute-start(f32[5,16,64]{2,1,0:T(8,128)S(1)} %slice_add_fusion.1), channel_id=1, source_target_pairs={{0,4},{4,0},{1,5},{5,1},{2,6},{6,2},{3,7},{7,3},{8,12},{12,8},{9,1... | collective-permute-start | bytes 61448 | tf_op jit(solution)/shard_map/ppermute | solution.py:18
  12.5 0.1 convolution_add_fusion.5
  12.6 1.4 %collective-permute-done.2 = f32[5,16,64]{2,1,0:T(8,128)S(1)} collective-permute-done((f32[5,16,64]{2,1,0:T(8,128)S(1)}, f32[5,16,64]{2,1,0:T(8,128)S(1)}, u32[]{:S(2)}, u32[]{:S(2)}) %collective-permute-start.2) | collective-permute-done | bytes 20512 | tf_op jit(solution)/shard_map/ppermute | solution.py:18
  14.0 1.7 %collective-permute-start.3 = (f32[4,16,64]{2,1,0:T(8,128)S(1)}, f32[4,16,64]{2,1,0:T(8,128)S(1)}, u32[]{:S(2)}, u32[]{:S(2)}) collective-permute-start(f32[4,16,64]{2,1,0:T(8,128)S(1)} %slice_add_fusion.2), channel_id=1, source_target_pairs={{0,8},{8,0},{1,9},{9,1},{2,10},{10,2},{3,11},{11,3},{4,12},{12,4},... | collective-permute-start | bytes 49160 | tf_op jit(solution)/shard_map/ppermute | solution.py:18
  15.8 0.1 convolution_add_fusion.4
  15.9 1.2 %collective-permute-done.3 = f32[4,16,64]{2,1,0:T(8,128)S(1)} collective-permute-done((f32[4,16,64]{2,1,0:T(8,128)S(1)}, f32[4,16,64]{2,1,0:T(8,128)S(1)}, u32[]{:S(2)}, u32[]{:S(2)}) %collective-permute-start.3) | collective-permute-done | bytes 16416 | tf_op jit(solution)/shard_map/ppermute | solution.py:18
  17.1 3.4 %collective-permute-start.4 = (f32[3,16,64]{2,1,0:T(8,128)S(1)}, f32[3,16,64]{2,1,0:T(8,128)S(1)}, u32[]{:S(2)}, u32[]{:S(2)}) collective-permute-start(f32[3,16,64]{2,1,0:T(8,128)S(1)} %slice_add_fusion.3), channel_id=1, source_target_pairs={{0,16},{16,0},{1,17},{17,1},{2,18},{18,2},{3,19},{19,3},{4,20},{20... | collective-permute-start | bytes 36872 | tf_op jit(solution)/shard_map/ppermute | solution.py:18
  20.5 0.1 convolution_add_fusion.3
  20.6 1.1 %collective-permute-done.4 = f32[3,16,64]{2,1,0:T(8,128)S(1)} collective-permute-done((f32[3,16,64]{2,1,0:T(8,128)S(1)}, f32[3,16,64]{2,1,0:T(8,128)S(1)}, u32[]{:S(2)}, u32[]{:S(2)}) %collective-permute-start.4) | collective-permute-done | bytes 12320 | tf_op jit(solution)/shard_map/ppermute | solution.py:18
  21.7 1.3 %collective-permute-start.5 = (f32[2,16,64]{2,1,0:T(8,128)S(1)}, f32[2,16,64]{2,1,0:T(8,128)S(1)}, u32[]{:S(2)}, u32[]{:S(2)}) collective-permute-start(f32[2,16,64]{2,1,0:T(8,128)S(1)} %slice_add_fusion.4), channel_id=1, source_target_pairs={{0,32},{32,0},{1,33},{33,1},{2,34},{34,2},{3,35},{35,3},{4,36},{36... | collective-permute-start | bytes 24584 | tf_op jit(solution)/shard_map/ppermute | solution.py:18
  23.0 0.1 convolution_add_fusion.2
  23.1 1.4 %collective-permute-done.5 = f32[2,16,64]{2,1,0:T(8,128)S(1)} collective-permute-done((f32[2,16,64]{2,1,0:T(8,128)S(1)}, f32[2,16,64]{2,1,0:T(8,128)S(1)}, u32[]{:S(2)}, u32[]{:S(2)}) %collective-permute-start.5) | collective-permute-done | bytes 8224 | tf_op jit(solution)/shard_map/ppermute | solution.py:18
  24.6 2.9 %collective-permute-start.6 = (f32[1,16,64]{2,1,0:T(8,128)S(1)}, f32[1,16,64]{2,1,0:T(8,128)S(1)}, u32[]{:S(2)}, u32[]{:S(2)}) collective-permute-start(f32[1,16,64]{2,1,0:T(8,128)S(1)} %slice_add_fusion.5), channel_id=1, source_target_pairs={{0,64},{64,0},{1,65},{65,1},{2,66},{66,2},{3,67},{67,3},{4,68},{68... | collective-permute-start | bytes 12296 | tf_op jit(solution)/shard_map/ppermute | solution.py:18
  27.5 0.1 convolution_add_fusion.1
  27.6 1.0 collective-permute-done.6
  28.6 0.1 fusion.3
  28.7 0.3 convolution_multiply_fusion
  29.0 13.6 %psum.28 = f32[48,48]{0,1:T(8,128)S(1)} all-reduce(f32[48,48]{0,1:T(8,128)S(1)} %convolution_multiply_fusion), channel_id=1, replica_groups=mesh['gx_0'=4,'gx_1'=4,'gy_0'=4,'gy_1'=2] {'gx_0'}, use_global_device_ids=true, to_apply=%region_0.1 | all-reduce | flops 2304 | bytes 18432 | tf_op jit(solution)/shard_map/psum | solution.py:23
  42.6 14.2 %psum.29 = f32[48,48]{0,1:T(8,128)S(1)} all-reduce(f32[48,48]{0,1:T(8,128)S(1)} %psum.28), channel_id=1, replica_groups=mesh['gx_0'=4,'gx_1'=4,'gy_0'=4,'gy_1'=2] {'gx_1'}, use_global_device_ids=true, to_apply=%region_1.2 | all-reduce | flops 2304 | bytes 18432 | tf_op jit(solution)/shard_map/psum | solution.py:23
  56.8 13.3 %psum.30 = f32[48,48]{0,1:T(8,128)S(1)} all-reduce(f32[48,48]{0,1:T(8,128)S(1)} %psum.29), channel_id=1, replica_groups=mesh['gx_0'=4,'gx_1'=4,'gy_0'=4,'gy_1'=2] {'gy_0'}, use_global_device_ids=true, to_apply=%region_2.3 | all-reduce | flops 2304 | bytes 18432 | tf_op jit(solution)/shard_map/psum | solution.py:23
  70.1 20.4 %psum.31 = f32[48,48]{0,1:T(8,128)S(1)} all-reduce(f32[48,48]{0,1:T(8,128)S(1)} %psum.30), channel_id=1, replica_groups=mesh['gx_0'=4,'gx_1'=4,'gy_0'=4,'gy_1'=2] {'gy_1'}, use_global_device_ids=true, to_apply=%region_3.4 | all-reduce | flops 2304 | bytes 18432 | tf_op jit(solution)/shard_map/psum | solution.py:23
  90.5 0.2 convolution_subtract_fusion
  90.8 0.1 negate_bitcast_fusion
  90.8 0.2 fusion.2
  91.0 0.2 fusion.75
  91.2 0.2 fusion.74
  91.4 0.7 copy.11
  92.1 0.1 copy.10
  92.2 1.5 %cholesky.20 = f32[16,16]{1,0:T(8,128)S(1)} custom-call(f32[16,16]{1,0:T(8,128)S(1)} %fusion.38), custom_call_target="Cholesky" | custom-call | tf_op jit(solution)/shard_map/jit(cholesky)/cholesky | solution.py:76
  93.7 0.6 compare_reduce_fusion
  94.3 1.2 %select_bitcast_fusion = (f32[1,16,16]{2,1,0:T(8,128)S(1)}, f32[16,16]{1,0:T(8,128)}) fusion(f32[16,16]{1,0:T(8,128)S(1)} %cholesky.20, pred[]{:T(512)} %compare_reduce_fusion), kind=kLoop, calls=%fused_computation.66 | loop fusion | flops 1024 | bytes 3073 | tf_op jit(solution)/shard_map/jit(_solve_triangular)/triangular_solve | solution.py:77
  95.6 1.2 %custom-call.7 = f32[1,16,16]{1,2,0:T(8,128)S(1)} custom-call(f32[1,16,16]{2,1,0:T(8,128)S(1)} %get-tuple-element.6), custom_call_target="InvertDiagBlocksLowerTriangular" | custom-call | tf_op jit(solution)/shard_map/jit(_solve_triangular)/triangular_solve | solution.py:77
  96.8 0.9 fusion.36
  (12 shorter events, 0.1 us)
Async XLA Ops:
  0.6 4.1 %copy-start = (bf16[1,1024,1024]{2,1,0:T(8,128)(2,1)S(1)}, bf16[1,1024,1024]{2,1,0:T(8,128)(2,1)}, u32[]{:S(2)}) copy-start(bf16[1,1024,1024]{2,1,0:T(8,128)(2,1)} %param.9) | copy-start | bytes 6291460
  0.6 6.9 %copy-start.1 = (bf16[7,64,1024]{2,1,0:T(8,128)(2,1)S(1)}, bf16[7,64,1024]{2,1,0:T(8,128)(2,1)}, u32[]{:S(2)}) copy-start(bf16[7,64,1024]{2,1,0:T(8,128)(2,1)} %param.10) | copy-start | bytes 2752516
  0.7 5.4 %copy-start.2 = (bf16[16,1024]{1,0:T(8,128)(2,1)S(1)}, bf16[16,1024]{1,0:T(8,128)(2,1)}, u32[]{:S(2)}) copy-start(bf16[16,1024]{1,0:T(8,128)(2,1)} %param.6) | copy-start | bytes 98308
  0.7 5.4 %copy-start.3 = (bf16[16,1024]{1,0:T(8,128)(2,1)S(1)}, bf16[16,1024]{1,0:T(8,128)(2,1)}, u32[]{:S(2)}) copy-start(bf16[16,1024]{1,0:T(8,128)(2,1)} %param.7) | copy-start | bytes 98308
  0.7 5.5 %copy-start.4 = (f32[16,16]{1,0:T(8,128)S(1)}, f32[16,16]{1,0:T(8,128)}, u32[]{:S(2)}) copy-start(f32[16,16]{1,0:T(8,128)} %param.8) | copy-start | bytes 3076
  3.2 2.9 %collective-permute-start = (f32[7,16,64]{2,1,0:T(8,128)S(1)}, f32[7,16,64]{2,1,0:T(8,128)S(1)}, u32[]{:S(2)}, u32[]{:S(2)}) collective-permute-start(f32[7,16,64]{2,1,0:T(8,128)S(1)} %convolution_bitcast_fusion.1), channel_id=1, source_target_pairs={{0,1},{1,0},{2,3},{3,2},{4,5},{5,4},{6,7},{7,6},{8,9},{9,8},{10,11... | collective-permute-start | bytes 86024 | tf_op jit(solution)/shard_map/ppermute | solution.py:18
  6.2 3.5 %collective-permute-start.1 = (f32[6,16,64]{2,1,0:T(8,128)S(1)}, f32[6,16,64]{2,1,0:T(8,128)S(1)}, u32[]{:S(2)}, u32[]{:S(2)}) collective-permute-start(f32[6,16,64]{2,1,0:T(8,128)S(1)} %slice_add_fusion), channel_id=1, source_target_pairs={{0,2},{2,0},{1,3},{3,1},{4,6},{6,4},{5,7},{7,5},{8,10},{10,8},{9,1... | collective-permute-start | bytes 73736 | tf_op jit(solution)/shard_map/ppermute | solution.py:18
  9.7 4.4 %collective-permute-start.2 = (f32[5,16,64]{2,1,0:T(8,128)S(1)}, f32[5,16,64]{2,1,0:T(8,128)S(1)}, u32[]{:S(2)}, u32[]{:S(2)}) collective-permute-start(f32[5,16,64]{2,1,0:T(8,128)S(1)} %slice_add_fusion.1), channel_id=1, source_target_pairs={{0,4},{4,0},{1,5},{5,1},{2,6},{6,2},{3,7},{7,3},{8,12},{12,8},{9,1... | collective-permute-start | bytes 61448 | tf_op jit(solution)/shard_map/ppermute | solution.py:18
  14.0 3.0 %collective-permute-start.3 = (f32[4,16,64]{2,1,0:T(8,128)S(1)}, f32[4,16,64]{2,1,0:T(8,128)S(1)}, u32[]{:S(2)}, u32[]{:S(2)}) collective-permute-start(f32[4,16,64]{2,1,0:T(8,128)S(1)} %slice_add_fusion.2), channel_id=1, source_target_pairs={{0,8},{8,0},{1,9},{9,1},{2,10},{10,2},{3,11},{11,3},{4,12},{12,4},... | collective-permute-start | bytes 49160 | tf_op jit(solution)/shard_map/ppermute | solution.py:18
  17.1 4.6 %collective-permute-start.4 = (f32[3,16,64]{2,1,0:T(8,128)S(1)}, f32[3,16,64]{2,1,0:T(8,128)S(1)}, u32[]{:S(2)}, u32[]{:S(2)}) collective-permute-start(f32[3,16,64]{2,1,0:T(8,128)S(1)} %slice_add_fusion.3), channel_id=1, source_target_pairs={{0,16},{16,0},{1,17},{17,1},{2,18},{18,2},{3,19},{19,3},{4,20},{20... | collective-permute-start | bytes 36872 | tf_op jit(solution)/shard_map/ppermute | solution.py:18
  21.7 2.9 %collective-permute-start.5 = (f32[2,16,64]{2,1,0:T(8,128)S(1)}, f32[2,16,64]{2,1,0:T(8,128)S(1)}, u32[]{:S(2)}, u32[]{:S(2)}) collective-permute-start(f32[2,16,64]{2,1,0:T(8,128)S(1)} %slice_add_fusion.4), channel_id=1, source_target_pairs={{0,32},{32,0},{1,33},{33,1},{2,34},{34,2},{3,35},{35,3},{4,36},{36... | collective-permute-start | bytes 24584 | tf_op jit(solution)/shard_map/ppermute | solution.py:18
  24.6 4.0 %collective-permute-start.6 = (f32[1,16,64]{2,1,0:T(8,128)S(1)}, f32[1,16,64]{2,1,0:T(8,128)S(1)}, u32[]{:S(2)}, u32[]{:S(2)}) collective-permute-start(f32[1,16,64]{2,1,0:T(8,128)S(1)} %slice_add_fusion.5), channel_id=1, source_target_pairs={{0,64},{64,0},{1,65},{65,1},{2,66},{66,2},{3,67},{67,3},{4,68},{68... | collective-permute-start | bytes 12296 | tf_op jit(solution)/shard_map/ppermute | solution.py:18
where the time goes:
time: 98 us; the launch traced here: 97.7 us
  blocking collectives  61.5 us (63%)
  starting transfers between devices  15 us (15%)
  waiting for transfers between devices  7.98 us (8%)
  matrix products  6.11 us (6%)
  other arithmetic  4.75 us (5%)
  between operations  1.58 us (2%)
    psum x4, blocking collectives, one_axis_at_a_time(): value = lax.psum(value, axis)  61.5 us
    ppermute x7, starting transfers between devices, partner_2(): return lax.ppermute(block, axis, route)  15 us
    ppermute x7, waiting for transfers between devices, partner_2(): return lax.ppermute(block, axis, route)  7.98 us
    another operation x2, other arithmetic, body(): next_block = jax.scipy.linalg.solve_triangular(factor, residual, lower=True)  2.47 us
    another operation x3, other arithmetic, body(): factor = jnp.linalg.cholesky(gram)  2.13 us
  transfers between devices with their start and end apart: 7, of which 6 were waited for; matrix products, arithmetic and copies ran while one was open for 2% of the time, Pallas kernels for 0%

commit v1 on v0

--- a/solution.py
+++ b/solution.py
@@ -20,7 +20,8 @@
 
 def one_axis_at_a_time(value, axes):
     for axis in axes:
-        value = lax.psum(value, axis)
+        shards = lax.all_gather(value, axis, axis=0, tiled=False)
+        value = shards.sum(axis=0)
     return value
 
 

time: 98 us -> 80.8 us (0.82)
  blocking collectives: 61.5 us -> 45 us
    psum x4 -> x0, blocking collectives: 61.5 us -> none  [one_axis_at_a_time(): value = lax.psum(value, axis)]
    all_gather x0 -> x4, blocking collectives: none -> 45 us  [one_axis_at_a_time(): shards = lax.all_gather(value, axis, axis=0, tiled=False)]
  transfers between devices with their start and end apart: 7 -> 7, of which waited for: 6 -> 6; matrix products, arithmetic and copies ran while one was open for 2% -> 3% of each run, Pallas kernels for 0% -> 0%
where the time goes in v1:
time: 80.8 us; the launch traced here: 80.6 us
  blocking collectives  45 us (56%)
  starting transfers between devices  15 us (19%)
  waiting for transfers between devices  7.98 us (10%)
  matrix products  6.1 us (8%)
  other arithmetic  4.75 us (6%)
  between operations  1.6 us (2%)
    all_gather x4, blocking collectives, one_axis_at_a_time(): shards = lax.all_gather(value, axis, axis=0, tiled=False)  45 us
    ppermute x7, starting transfers between devices, partner_2(): return lax.ppermute(block, axis, route)  15 us
    ppermute x7, waiting for transfers between devices, partner_2(): return lax.ppermute(block, axis, route)  7.98 us
    another operation x2, other arithmetic, body(): next_block = jax.scipy.linalg.solve_triangular(factor, residual, lower=True)  2.47 us
    another operation x3, other arithmetic, body(): factor = jnp.linalg.cholesky(gram)  2.15 us
    dot_general x1, matrix products, body(): jnp.einsum('pm,krm->kpr', block, bases, preferred_element_type=jnp.float32)  1.75 us
  transfers between devices with their start and end apart: 7, of which 6 were waited for; matrix products, arithmetic and copies ran while one was open for 3% of the time, Pallas kernels for 0%

profile of v1, /device:TPU:1, one launch (start us, length us, event | category | flops | bytes accessed | tf_op | source)
XLA Modules:
  0.0 80.6 jit_solution(17553134155703639016)
XLA Ops:
  0.6 0.0 copy-start
  0.6 0.0 copy-start.1
  0.7 0.0 copy-start.2
  0.7 0.0 copy-start.3
  0.7 0.0 copy-start.5
  1.5 1.7 %convolution_bitcast_fusion.1 = f32[7,16,64]{2,1,0:T(8,128)S(1)} fusion(bf16[7,64,1024]{2,1,0:T(8,128)(2,1)} %param.10, bf16[16,1024]{1,0:T(8,128)(2,1)} %param.6, pred[1024]{0:T(1024)(128)(4,1)S(1)} %iota_compare_fusion.2), kind=kOutput, calls=%fused_computation.13 | convolution fusion | flops 14696448 | bytes 979968 | tf_op jit(solution)/shard_map/pm,krm->kpr/dot_general | solution.py:56
  3.2 1.5 %collective-permute-start = (f32[7,16,64]{2,1,0:T(8,128)S(1)}, f32[7,16,64]{2,1,0:T(8,128)S(1)}, u32[]{:S(2)}, u32[]{:S(2)}) collective-permute-start(f32[7,16,64]{2,1,0:T(8,128)S(1)} %convolution_bitcast_fusion.1), channel_id=1, source_target_pairs={{0,1},{1,0},{2,3},{3,2},{4,5},{5,4},{6,7},{7,6},{8,9},{9,8},{10,11... | collective-permute-start | bytes 86024 | tf_op jit(solution)/shard_map/ppermute | solution.py:18
  4.7 0.0 copy-done
  4.7 1.4 %fusion = f32[16,1024]{1,0:T(8,128)S(1)} fusion(bf16[1,1024,1024]{2,1,0:T(8,128)(2,1)S(1)} %copy-done, bf16[16,1024]{1,0:T(8,128)(2,1)} %param.6, pred[1024]{0:T(1024)(128)(4,1)S(1)} %iota_compare_fusion.2), kind=kOutput, calls=%fused_computation | convolution fusion | flops 33570816 | bytes 2196480 | tf_op jit(solution)/shard_map/lrc,plc->plr/dot_general | solution.py:53
  6.1 0.0 copy-done.2
  6.1 0.0 copy-done.3
  6.2 0.0 copy-done.5
  6.2 0.0 collective-permute-done
  6.2 1.4 %collective-permute-start.1 = (f32[6,16,64]{2,1,0:T(8,128)S(1)}, f32[6,16,64]{2,1,0:T(8,128)S(1)}, u32[]{:S(2)}, u32[]{:S(2)}) collective-permute-start(f32[6,16,64]{2,1,0:T(8,128)S(1)} %slice_add_fusion), channel_id=1, source_target_pairs={{0,2},{2,0},{1,3},{3,1},{4,6},{6,4},{5,7},{7,5},{8,10},{10,8},{9,1... | collective-permute-start | bytes 73736 | tf_op jit(solution)/shard_map/ppermute | solution.py:18
  7.6 0.0 copy-done.1
  7.6 0.1 convolution_add_fusion.6
  7.7 1.9 %collective-permute-done.1 = f32[6,16,64]{2,1,0:T(8,128)S(1)} collective-permute-done((f32[6,16,64]{2,1,0:T(8,128)S(1)}, f32[6,16,64]{2,1,0:T(8,128)S(1)}, u32[]{:S(2)}, u32[]{:S(2)}) %collective-permute-start.1) | collective-permute-done | bytes 24608 | tf_op jit(solution)/shard_map/ppermute | solution.py:18
  9.7 2.8 %collective-permute-start.2 = (f32[5,16,64]{2,1,0:T(8,128)S(1)}, f32[5,16,64]{2,1,0:T(8,128)S(1)}, u32[]{:S(2)}, u32[]{:S(2)}) collective-permute-start(f32[5,16,64]{2,1,0:T(8,128)S(1)} %slice_add_fusion.1), channel_id=1, source_target_pairs={{0,4},{4,0},{1,5},{5,1},{2,6},{6,2},{3,7},{7,3},{8,12},{12,8},{9,1... | collective-permute-start | bytes 61448 | tf_op jit(solution)/shard_map/ppermute | solution.py:18
  12.5 0.1 convolution_add_fusion.5
  12.6 1.4 %collective-permute-done.2 = f32[5,16,64]{2,1,0:T(8,128)S(1)} collective-permute-done((f32[5,16,64]{2,1,0:T(8,128)S(1)}, f32[5,16,64]{2,1,0:T(8,128)S(1)}, u32[]{:S(2)}, u32[]{:S(2)}) %collective-permute-start.2) | collective-permute-done | bytes 20512 | tf_op jit(solution)/shard_map/ppermute | solution.py:18
  14.0 1.7 %collective-permute-start.3 = (f32[4,16,64]{2,1,0:T(8,128)S(1)}, f32[4,16,64]{2,1,0:T(8,128)S(1)}, u32[]{:S(2)}, u32[]{:S(2)}) collective-permute-start(f32[4,16,64]{2,1,0:T(8,128)S(1)} %slice_add_fusion.2), channel_id=1, source_target_pairs={{0,8},{8,0},{1,9},{9,1},{2,10},{10,2},{3,11},{11,3},{4,12},{12,4},... | collective-permute-start | bytes 49160 | tf_op jit(solution)/shard_map/ppermute | solution.py:18
  15.8 0.1 convolution_add_fusion.4
  15.9 1.2 %collective-permute-done.3 = f32[4,16,64]{2,1,0:T(8,128)S(1)} collective-permute-done((f32[4,16,64]{2,1,0:T(8,128)S(1)}, f32[4,16,64]{2,1,0:T(8,128)S(1)}, u32[]{:S(2)}, u32[]{:S(2)}) %collective-permute-start.3) | collective-permute-done | bytes 16416 | tf_op jit(solution)/shard_map/ppermute | solution.py:18
  17.1 3.4 %collective-permute-start.4 = (f32[3,16,64]{2,1,0:T(8,128)S(1)}, f32[3,16,64]{2,1,0:T(8,128)S(1)}, u32[]{:S(2)}, u32[]{:S(2)}) collective-permute-start(f32[3,16,64]{2,1,0:T(8,128)S(1)} %slice_add_fusion.3), channel_id=1, source_target_pairs={{0,16},{16,0},{1,17},{17,1},{2,18},{18,2},{3,19},{19,3},{4,20},{20... | collective-permute-start | bytes 36872 | tf_op jit(solution)/shard_map/ppermute | solution.py:18
  20.5 0.1 convolution_add_fusion.3
  20.6 1.1 %collective-permute-done.4 = f32[3,16,64]{2,1,0:T(8,128)S(1)} collective-permute-done((f32[3,16,64]{2,1,0:T(8,128)S(1)}, f32[3,16,64]{2,1,0:T(8,128)S(1)}, u32[]{:S(2)}, u32[]{:S(2)}) %collective-permute-start.4) | collective-permute-done | bytes 12320 | tf_op jit(solution)/shard_map/ppermute | solution.py:18
  21.7 1.3 %collective-permute-start.5 = (f32[2,16,64]{2,1,0:T(8,128)S(1)}, f32[2,16,64]{2,1,0:T(8,128)S(1)}, u32[]{:S(2)}, u32[]{:S(2)}) collective-permute-start(f32[2,16,64]{2,1,0:T(8,128)S(1)} %slice_add_fusion.4), channel_id=1, source_target_pairs={{0,32},{32,0},{1,33},{33,1},{2,34},{34,2},{3,35},{35,3},{4,36},{36... | collective-permute-start | bytes 24584 | tf_op jit(solution)/shard_map/ppermute | solution.py:18
  23.0 0.1 convolution_add_fusion.2
  23.1 1.5 %collective-permute-done.5 = f32[2,16,64]{2,1,0:T(8,128)S(1)} collective-permute-done((f32[2,16,64]{2,1,0:T(8,128)S(1)}, f32[2,16,64]{2,1,0:T(8,128)S(1)}, u32[]{:S(2)}, u32[]{:S(2)}) %collective-permute-start.5) | collective-permute-done | bytes 8224 | tf_op jit(solution)/shard_map/ppermute | solution.py:18
  24.6 2.9 %collective-permute-start.6 = (f32[1,16,64]{2,1,0:T(8,128)S(1)}, f32[1,16,64]{2,1,0:T(8,128)S(1)}, u32[]{:S(2)}, u32[]{:S(2)}) collective-permute-start(f32[1,16,64]{2,1,0:T(8,128)S(1)} %slice_add_fusion.5), channel_id=1, source_target_pairs={{0,64},{64,0},{1,65},{65,1},{2,66},{66,2},{3,67},{67,3},{4,68},{68... | collective-permute-start | bytes 12296 | tf_op jit(solution)/shard_map/ppermute | solution.py:18
  27.5 0.1 convolution_add_fusion.1
  27.6 1.0 %collective-permute-done.6 = f32[1,16,64]{2,1,0:T(8,128)S(1)} collective-permute-done((f32[1,16,64]{2,1,0:T(8,128)S(1)}, f32[1,16,64]{2,1,0:T(8,128)S(1)}, u32[]{:S(2)}, u32[]{:S(2)}) %collective-permute-start.6) | collective-permute-done | bytes 4128 | tf_op jit(solution)/shard_map/ppermute | solution.py:18
  28.6 0.1 fusion.3
  28.7 0.3 convolution_multiply_fusion
  29.1 9.8 %all-gather = f32[192,48]{1,0:T(8,128)S(1)} all-gather(f32[48,48]{1,0:T(8,128)S(1)} %convolution_multiply_fusion), channel_id=2, replica_groups=mesh['gx_0'=4,'gx_1'=4,'gy_0'=4,'gy_1'=2] {'gx_0'}, dimensions={0}, use_global_device_ids=true | all-gather | bytes 46080 | tf_op jit(solution)/shard_map/all_gather | solution.py:23
  38.9 9.5 %all-gather.1 = f32[192,48]{1,0:T(8,128)S(1)} all-gather(f32[48,48]{1,0:T(8,128)S(1)} %reduce_sum.36), channel_id=3, replica_groups=mesh['gx_0'=4,'gx_1'=4,'gy_0'=4,'gy_1'=2] {'gx_1'}, dimensions={0}, use_global_device_ids=true | all-gather | bytes 46080 | tf_op jit(solution)/shard_map/all_gather | solution.py:23
  48.4 9.7 %all-gather.2 = f32[192,48]{1,0:T(8,128)S(1)} all-gather(f32[48,48]{1,0:T(8,128)S(1)} %reduce_sum.37), channel_id=4, replica_groups=mesh['gx_0'=4,'gx_1'=4,'gy_0'=4,'gy_1'=2] {'gy_0'}, dimensions={0}, use_global_device_ids=true | all-gather | bytes 46080 | tf_op jit(solution)/shard_map/all_gather | solution.py:23
  58.1 15.9 %all-gather.3 = f32[96,48]{1,0:T(8,128)S(1)} all-gather(f32[48,48]{1,0:T(8,128)S(1)} %reduce_sum.38), channel_id=5, replica_groups=mesh['gx_0'=4,'gx_1'=4,'gy_0'=4,'gy_1'=2] {'gy_1'}, dimensions={0}, use_global_device_ids=true | all-gather | bytes 27648 | tf_op jit(solution)/shard_map/all_gather | solution.py:23
  74.1 0.0 copy-start.4
  74.1 0.2 convolution_subtract_fusion
  74.3 0.1 copy.14
  74.4 0.2 fusion.2
  74.6 0.2 fusion.74
  74.8 0.2 fusion.73
  75.0 0.1 copy.12
  75.1 1.5 %cholesky.20 = f32[16,16]{1,0:T(8,128)S(1)} custom-call(f32[16,16]{1,0:T(8,128)S(1)} %fusion.38), custom_call_target="Cholesky" | custom-call | tf_op jit(solution)/shard_map/jit(cholesky)/cholesky | solution.py:77
  76.6 0.6 compare_reduce_fusion
  77.2 1.2 %select_bitcast_fusion = (f32[1,16,16]{2,1,0:T(8,128)S(1)}, f32[16,16]{1,0:T(8,128)}) fusion(f32[16,16]{1,0:T(8,128)S(1)} %cholesky.20, pred[]{:T(512)} %compare_reduce_fusion), kind=kLoop, calls=%fused_computation.66 | loop fusion | flops 1024 | bytes 3073 | tf_op jit(solution)/shard_map/jit(_solve_triangular)/triangular_solve | solution.py:78
  78.5 1.2 %custom-call.7 = f32[1,16,16]{1,2,0:T(8,128)S(1)} custom-call(f32[1,16,16]{2,1,0:T(8,128)S(1)} %get-tuple-element.9), custom_call_target="InvertDiagBlocksLowerTriangular" | custom-call | tf_op jit(solution)/shard_map/jit(_solve_triangular)/triangular_solve | solution.py:78
  79.7 0.9 %fusion.36 = f32[16,1024]{1,0:T(8,128)} fusion(f32[16,1024]{1,0:T(8,128)S(1)} %fusion.2, f32[1,16,16]{1,2,0:T(8,128)S(1)} %custom-call.7), kind=kOutput, calls=%fused_computation.62 | convolution fusion | flops 3145728 | bytes 132096 | tf_op jit(solution)/shard_map/jit(_solve_triangular)/triangular_solve | solution.py:78
  80.6 0.0 copy-done.4
  (18 shorter events, 0.2 us)
Async XLA Ops:
  0.6 4.1 %copy-start = (bf16[1,1024,1024]{2,1,0:T(8,128)(2,1)S(1)}, bf16[1,1024,1024]{2,1,0:T(8,128)(2,1)}, u32[]{:S(2)}) copy-start(bf16[1,1024,1024]{2,1,0:T(8,128)(2,1)} %param.9) | copy-start | bytes 6291460
  0.6 6.9 %copy-start.1 = (bf16[7,64,1024]{2,1,0:T(8,128)(2,1)S(1)}, bf16[7,64,1024]{2,1,0:T(8,128)(2,1)}, u32[]{:S(2)}) copy-start(bf16[7,64,1024]{2,1,0:T(8,128)(2,1)} %param.10) | copy-start | bytes 2752516
  0.7 5.4 %copy-start.2 = (bf16[16,1024]{1,0:T(8,128)(2,1)S(1)}, bf16[16,1024]{1,0:T(8,128)(2,1)}, u32[]{:S(2)}) copy-start(bf16[16,1024]{1,0:T(8,128)(2,1)} %param.6) | copy-start | bytes 98308
  0.7 5.4 %copy-start.3 = (bf16[16,1024]{1,0:T(8,128)(2,1)S(1)}, bf16[16,1024]{1,0:T(8,128)(2,1)}, u32[]{:S(2)}) copy-start(bf16[16,1024]{1,0:T(8,128)(2,1)} %param.7) | copy-start | bytes 98308
  0.7 5.5 %copy-start.5 = (f32[16,16]{1,0:T(8,128)S(1)}, f32[16,16]{1,0:T(8,128)}, u32[]{:S(2)}) copy-start(f32[16,16]{1,0:T(8,128)} %param.8) | copy-start | bytes 3076
  3.2 2.9 %collective-permute-start = (f32[7,16,64]{2,1,0:T(8,128)S(1)}, f32[7,16,64]{2,1,0:T(8,128)S(1)}, u32[]{:S(2)}, u32[]{:S(2)}) collective-permute-start(f32[7,16,64]{2,1,0:T(8,128)S(1)} %convolution_bitcast_fusion.1), channel_id=1, source_target_pairs={{0,1},{1,0},{2,3},{3,2},{4,5},{5,4},{6,7},{7,6},{8,9},{9,8},{10,11... | collective-permute-start | bytes 86024 | tf_op jit(solution)/shard_map/ppermute | solution.py:18
  6.2 3.5 %collective-permute-start.1 = (f32[6,16,64]{2,1,0:T(8,128)S(1)}, f32[6,16,64]{2,1,0:T(8,128)S(1)}, u32[]{:S(2)}, u32[]{:S(2)}) collective-permute-start(f32[6,16,64]{2,1,0:T(8,128)S(1)} %slice_add_fusion), channel_id=1, source_target_pairs={{0,2},{2,0},{1,3},{3,1},{4,6},{6,4},{5,7},{7,5},{8,10},{10,8},{9,1... | collective-permute-start | bytes 73736 | tf_op jit(solution)/shard_map/ppermute | solution.py:18
  9.7 4.4 %collective-permute-start.2 = (f32[5,16,64]{2,1,0:T(8,128)S(1)}, f32[5,16,64]{2,1,0:T(8,128)S(1)}, u32[]{:S(2)}, u32[]{:S(2)}) collective-permute-start(f32[5,16,64]{2,1,0:T(8,128)S(1)} %slice_add_fusion.1), channel_id=1, source_target_pairs={{0,4},{4,0},{1,5},{5,1},{2,6},{6,2},{3,7},{7,3},{8,12},{12,8},{9,1... | collective-permute-start | bytes 61448 | tf_op jit(solution)/shard_map/ppermute | solution.py:18
  14.0 3.0 %collective-permute-start.3 = (f32[4,16,64]{2,1,0:T(8,128)S(1)}, f32[4,16,64]{2,1,0:T(8,128)S(1)}, u32[]{:S(2)}, u32[]{:S(2)}) collective-permute-start(f32[4,16,64]{2,1,0:T(8,128)S(1)} %slice_add_fusion.2), channel_id=1, source_target_pairs={{0,8},{8,0},{1,9},{9,1},{2,10},{10,2},{3,11},{11,3},{4,12},{12,4},... | collective-permute-start | bytes 49160 | tf_op jit(solution)/shard_map/ppermute | solution.py:18
  17.1 4.6 %collective-permute-start.4 = (f32[3,16,64]{2,1,0:T(8,128)S(1)}, f32[3,16,64]{2,1,0:T(8,128)S(1)}, u32[]{:S(2)}, u32[]{:S(2)}) collective-permute-start(f32[3,16,64]{2,1,0:T(8,128)S(1)} %slice_add_fusion.3), channel_id=1, source_target_pairs={{0,16},{16,0},{1,17},{17,1},{2,18},{18,2},{3,19},{19,3},{4,20},{20... | collective-permute-start | bytes 36872 | tf_op jit(solution)/shard_map/ppermute | solution.py:18
  21.7 2.9 %collective-permute-start.5 = (f32[2,16,64]{2,1,0:T(8,128)S(1)}, f32[2,16,64]{2,1,0:T(8,128)S(1)}, u32[]{:S(2)}, u32[]{:S(2)}) collective-permute-start(f32[2,16,64]{2,1,0:T(8,128)S(1)} %slice_add_fusion.4), channel_id=1, source_target_pairs={{0,32},{32,0},{1,33},{33,1},{2,34},{34,2},{3,35},{35,3},{4,36},{36... | collective-permute-start | bytes 24584 | tf_op jit(solution)/shard_map/ppermute | solution.py:18
  24.6 4.0 %collective-permute-start.6 = (f32[1,16,64]{2,1,0:T(8,128)S(1)}, f32[1,16,64]{2,1,0:T(8,128)S(1)}, u32[]{:S(2)}, u32[]{:S(2)}) collective-permute-start(f32[1,16,64]{2,1,0:T(8,128)S(1)} %slice_add_fusion.5), channel_id=1, source_target_pairs={{0,64},{64,0},{1,65},{65,1},{2,66},{66,2},{3,67},{67,3},{4,68},{68... | collective-permute-start | bytes 12296 | tf_op jit(solution)/shard_map/ppermute | solution.py:18
  74.1 6.5 %copy-start.4 = (f32[16,16]{1,0:T(8,128)}, f32[16,16]{1,0:T(8,128)S(1)}, u32[]{:S(2)}) copy-start(f32[16,16]{1,0:T(8,128)S(1)} %slice.134) | copy-start | bytes 3076
